TPU v7x, 32 devices: a whole 2x2x4 slice. The times are simulated.
32 devices in a mesh: flow: 2 (over x), col: 4 (over y, core), row: 4 (over z).
Axes of the slice: x: 2, y: 2, z: 4, core: 2. Of those that a mesh axis runs over, the one named last changes fastest.
Arguments:
- forcing: float32 [5, 12, 48, 768], P(None, 'flow', 'col', 'row'), may hold values from -6 to 6
- previous: float32 [5, 12, 48, 768], P(None, 'flow', 'col', 'row'), may hold values from -6 to 6
- element_diagonal_shift: float32 [2, 8, 128], P('flow', 'col', 'row'), may hold values from 0.5 to 4
- eigen_bases: float32 [3, 6, 6], replicated, may hold values from -1 to 1, as said below
- eigen_values: float32 [3, 6], replicated, may hold values from 0.5 to 8
- observers: float32 [3, 256], replicated, may hold values from 8 to 30
- panel_points: float32 [3, 1024], P(None, ('flow', 'col', 'row')), may hold values from -2 to 2
- surface_history: float32 [4, 15, 1024], P(None, None, ('flow', 'col', 'row')), may hold values from -6 to 6
Outputs:
- new_state: float32 [5, 12, 48, 768], P(None, 'flow', 'col', 'row')
- spectra: float32 [2, 16, 256], P(None, None, 'row')
Inputs may be any that keep to these rules, and one draw needn't show every extreme that they name: Each eigen_bases[d] is an orthogonal matrix.
All inputs are finite; a program needn't handle non-finite values.
Results may differ from a plain program's by a relative error of at most 0.0003.
Values sent between devices are 32-bit elements; how exact they have to be, the bound alone decides.
A program may use at most 64 MiB of HBM per device.

v0:
```python
import math
import jax
import jax.numpy as jnp
from jax import lax
from jax.sharding import PartitionSpec as P

P_SIZE = 6
SWEEPS = 2
NT = 16
NF = 16
HIGH = lax.Precision.HIGHEST
OMEGA = 0.8
TAU = 0.5
KMAX = 2.0


def with_halo(x, sides, width):
    for axis, dim in sides:
        size, length = (lax.axis_size(axis), x.shape[dim])
        up = [(i, (i + 1) % size) for i in range(size - 1)]
        down = [(j, i) for i, j in up]
        last = lax.slice_in_dim(x, length - width, length, axis=dim)
        first = lax.slice_in_dim(x, 0, width, axis=dim)
        before = lax.ppermute(last, axis, up)
        after = lax.ppermute(first, axis, down)
        x = jnp.concatenate([before, x, after], axis=dim)
    return x


def contract_small(field, matrix, which):
    extent = field.shape
    count = extent[which]
    blocked = field.reshape(extent[:which] + (count // P_SIZE, P_SIZE) + extent[which + 1 :])
    blocked = jnp.moveaxis(blocked, which + 1, -1)
    result = jnp.einsum("...p,qp->...q", blocked, matrix, precision=HIGH)
    result = jnp.moveaxis(result, -1, which + 1)
    return result.reshape(extent)


def contract_last(field, wide_matrix):
    extent = field.shape
    group = wide_matrix.shape[0]
    blocked = field.reshape(extent[0], extent[1], extent[2], extent[3] // group, group)
    result = jnp.einsum("cxybg,hg->cxybh", blocked, wide_matrix, precision=HIGH)
    return result.reshape(extent)


def face_masks(count):
    index = jnp.arange(count) % P_SIZE
    return ((index == P_SIZE - 1).astype(jnp.float32), (index == 0).astype(jnp.float32))


def far_terms(observers, points, source_re, source_im):
    offsets = observers[:, :, None] - points[:, None, :]
    radius = jnp.sqrt(jnp.sum(offsets * offsets, axis=0))
    unit_dir = offsets / radius[None]
    freqs = source_re.shape[1]
    wavenum = (KMAX * (jnp.arange(freqs, dtype=jnp.float32) + 0.5) / freqs)[:, None, None]
    along_re = (
        unit_dir[0][None] * source_re[1][:, None, :]
        + unit_dir[1][None] * source_re[2][:, None, :]
        + unit_dir[2][None] * source_re[3][:, None, :]
    )
    along_im = (
        unit_dir[0][None] * source_im[1][:, None, :]
        + unit_dir[1][None] * source_im[2][:, None, :]
        + unit_dir[2][None] * source_im[3][:, None, :]
    )
    inverse_matrix = 1.0 / radius[None]
    term_re = -wavenum * (source_im[0][:, None, :] + along_im) + along_re * inverse_matrix
    term_im = wavenum * (source_re[0][:, None, :] + along_re) + along_im * inverse_matrix
    phases = wavenum * radius[None]
    amplitude = inverse_matrix / (4.0 * math.pi)
    green_re = amplitude * jnp.cos(phases)
    green_im = -amplitude * jnp.sin(phases)
    total_re = jnp.sum(green_re * term_re - green_im * term_im, axis=2)
    total_im = jnp.sum(green_re * term_im + green_im * term_re, axis=2)
    return jnp.stack([total_re, total_im])


def transform(samples):
    times = jnp.arange(NT, dtype=jnp.float32)
    omegas = math.pi * (jnp.arange(NF, dtype=jnp.float32) + 0.5) / NF
    cos_table = jnp.cos(omegas[:, None] * times[None, :])
    sin_table = jnp.sin(omegas[:, None] * times[None, :])
    source_re = jnp.einsum("fn,cnp->cfp", cos_table, samples, precision=HIGH)
    source_im = -jnp.einsum("fn,cnp->cfp", sin_table, samples, precision=HIGH)
    return (source_re, source_im)


def on_device(
    forcing,
    previous,
    element_diagonal_shift,
    eigen_bases,
    eigen_values,
    observers,
    panel_points,
    surface_history,
):
    extent = forcing.shape
    stiffness = [
        jnp.dot(
            eigen_bases[axis_num] * eigen_values[axis_num][None, :],
            eigen_bases[axis_num].T,
            precision=HIGH,
        )
        for axis_num in range(3)
    ]
    group = P_SIZE * math.gcd(extent[3] // P_SIZE, 64)
    identity = jnp.eye(group // P_SIZE, dtype=jnp.float32)
    wide_stiff = jnp.kron(identity, stiffness[2])
    wide_forward = jnp.kron(identity, eigen_bases[2].T)
    wide_back = jnp.kron(identity, eigen_bases[2])
    shift_nodes = jnp.repeat(
        jnp.repeat(jnp.repeat(element_diagonal_shift, P_SIZE, 0), P_SIZE, 1), P_SIZE, 2
    )
    denominator = (
        shift_nodes
        + jnp.tile(eigen_values[0], extent[1] // P_SIZE)[:, None, None]
        + jnp.tile(eigen_values[1], extent[2] // P_SIZE)[None, :, None]
        + jnp.tile(eigen_values[2], extent[3] // P_SIZE)[None, None, :]
    )
    high_x, low_x = face_masks(extent[1])
    high_y, low_y = face_masks(extent[2])
    high_z, low_z = face_masks(extent[3])
    state = previous
    for sweep in range(SWEEPS):
        apply_result = shift_nodes[None] * state + contract_small(state, stiffness[0], 1)
        apply_result = apply_result + contract_small(state, stiffness[1], 2)
        padded = with_halo(state, (("flow", 1), ("col", 2), ("row", 3)), 1)
        next_x = padded[:, 2:, 1:-1, 1:-1]
        prev_x = padded[:, :-2, 1:-1, 1:-1]
        next_y = padded[:, 1:-1, 2:, 1:-1]
        prev_y = padded[:, 1:-1, :-2, 1:-1]
        next_z = padded[:, 1:-1, 1:-1, 2:]
        prev_z = padded[:, 1:-1, 1:-1, :-2]
        result = high_x[None, :, None, None] * next_x + low_x[None, :, None, None] * prev_x
        result = result + high_y[None, None, :, None] * next_y + low_y[None, None, :, None] * prev_y
        residual = (
            forcing
            - (apply_result + contract_last(state, wide_stiff))
            + TAU
            * (result + high_z[None, None, None, :] * next_z + low_z[None, None, None, :] * prev_z)
        )
        block_result = contract_small(residual, eigen_bases[0].T, 1)
        block_result = contract_small(block_result, eigen_bases[1].T, 2)
        block_result = contract_last(block_result, wide_forward) / denominator[None]
        block_result = contract_small(block_result, eigen_bases[0], 1)
        block_result = contract_small(block_result, eigen_bases[1], 2)
        state = state + OMEGA * contract_last(block_result, wide_back)
    own_panels = panel_points.shape[1]
    newest = state[:4, 0, 0, :own_panels]
    surface_samples = jnp.concatenate([surface_history, newest[:, None, :]], axis=1)
    rows = lax.axis_size("row")
    count = observers.shape[1] // rows
    points, samples = (
        lax.all_gather(panel_points, "row", axis=1, tiled=True),
        lax.all_gather(surface_samples, "row", axis=2, tiled=True),
    )
    source_re, source_im = transform(samples)
    own_obs = lax.dynamic_slice_in_dim(observers, lax.axis_index("row") * count, count, 1)
    partial_sums = far_terms(own_obs, points, source_re, source_im)
    spectra = lax.psum(partial_sums, ("flow", "col"))
    return (state, spectra)


def solution(mesh):
    return jax.shard_map(
        on_device,
        mesh=mesh,
        in_specs=(
            P(None, "flow", "col", "row"),
            P(None, "flow", "col", "row"),
            P("flow", "col", "row"),
            P(),
            P(),
            P(),
            P(None, ("flow", "col", "row")),
            P(None, None, ("flow", "col", "row")),
        ),
        out_specs=(P(None, "flow", "col", "row"), P(None, None, "row")),
        check_vma=False,
    )
```

profile of v0, /device:TPU:0, one launch (start us, length us, event | category | flops | bytes accessed | tf_op | source)
XLA Modules:
  0.0 143.8 jit_solution(3606890502460777156)
XLA Ops:
  0.6 0.9 fusion.168
  1.7 1.3 collective-permute-start
  3.0 4.8 %collective-permute-start.1 = (f32[5,1,12,192]{3,1,2,0:T(1,128)S(1)}, f32[5,1,12,192]{3,1,2,0:T(1,128)S(1)}, u32[]{:S(2)}, u32[]{:S(2)}) collective-permute-start(f32[5,1,12,192]{3,1,2,0:T(1,128)S(1)} %copy.139), channel_id=1, source_target_pairs={{0,16},{1,17},{2,18},{3,19},{4,20},{5,21},{6,22},{7,23},{8,24},{9,... | collective-permute-start | bytes 138248 | tf_op jit(solution)/shard_map/ppermute | solution.py:24
  7.9 1.3 copy.153
  10.8 0.9 fusion.131
  11.7 4.9 %broadcast_multiply_fusion = (f32[32,6,32,6]{3,2,1,0:T(8,128)}, f32[32,6,32,6]{3,2,1,0:T(8,128)}, f32[32,6,32,6]{3,2,1,0:T(8,128)}) fusion(f32[6,6]{1,0:T(8,128)S(1)} %get-tuple-element.42, f32[32,32]{1,0:T(8,128)S(1)} %fusion.118, f32[6,6]{1,0:T(8,128)S(1)} %copy.146, f32[6,6]{1,0:T(8,128)S(1)} %fusion.131), kind=kLoop, calls=%fused_computation | loop fusion | flops 110592 | bytes 446896 | tf_op jit(solution)/shard_map/jit(kron)/mul | solution.py:114
  16.6 3.9 %reshape.301 = f32[192,192,1,1]{1,0,2,3:T(8,128)S(1)} reshape(f32[32,6,32,6]{3,2,1,0:T(8,128)} %get-tuple-element.41) | data formatting | bytes 294912 | tf_op jit(solution)/shard_map/jit(kron)/mul | solution.py:112
  22.9 13.2 %all-gather = f32[4,32,3]{1,2,0:T(4,128)S(1)} all-gather(f32[1,32,3]{1,2,0:T(4,128)S(1)} %bitcast.282), channel_id=1, replica_groups=mesh['flow'=2,'col'=4,'row'=4] {'row'}, dimensions={0}, use_global_device_ids=true | all-gather | bytes 1920 | tf_op jit(solution)/shard_map/all_gather | solution.py:158
  38.5 1.1 fusion.3
  39.7 1.3 collective-permute-start.2
  41.0 3.0 %collective-permute-start.3 = (f32[5,8,1,192]{3,1,2,0:T(8,128)S(1)}, f32[5,8,1,192]{3,1,2,0:T(8,128)S(1)}, u32[]{:S(2)}, u32[]{:S(2)}) collective-permute-start(f32[5,8,1,192]{3,1,2,0:T(8,128)S(1)} %get-tuple-element.14), channel_id=1, source_target_pairs={{0,4},{4,8},{8,12},{1,5},{5,9},{9,13},{2,6},{6,10},{10,14},{3,7},{... | collective-permute-start | bytes 92168 | tf_op jit(solution)/shard_map/ppermute | solution.py:24
  44.1 0.8 collective-permute-done.3
  45.3 4.2 %collective-permute-start.5 = (f32[5,8,14,1]{3,1,2,0:T(8,128)S(1)}, f32[5,8,14,1]{3,1,2,0:T(8,128)}, u32[]{:S(2)}, u32[]{:S(2)}) collective-permute-start(f32[5,8,14,1]{3,1,2,0:T(8,128)S(1)} %get-tuple-element.19), channel_id=1, source_target_pairs={{0,1},{1,2},{2,3},{4,5},{5,6},{6,7},{8,9},{9,10},{10,11},{12,13},{... | collective-permute-start | bytes 6728 | tf_op jit(solution)/shard_map/ppermute | solution.py:24
  49.5 1.5 %collective-permute-start.4 = (f32[5,8,14,1]{3,1,2,0:T(8,128)S(1)}, f32[5,8,14,1]{3,1,2,0:T(8,128)}, u32[]{:S(2)}, u32[]{:S(2)}) collective-permute-start(f32[5,8,14,1]{3,1,2,0:T(8,128)S(1)} %get-tuple-element.18), channel_id=1, source_target_pairs={{1,0},{2,1},{3,2},{5,4},{6,5},{7,6},{9,8},{10,9},{11,10},{13,12},{... | collective-permute-start | bytes 6728 | tf_op jit(solution)/shard_map/ppermute | solution.py:25
  51.0 3.9 %reshape.304 = f32[192,192,1,1]{1,0,2,3:T(8,128)S(1)} reshape(f32[32,6,32,6]{3,2,1,0:T(8,128)} %get-tuple-element.40) | data formatting | bytes 294912 | tf_op jit(solution)/shard_map/jit(kron)/mul | solution.py:113
  54.8 3.9 %reshape.307 = f32[192,192,1,1]{1,0,2,3:T(8,128)S(1)} reshape(f32[32,6,32,6]{3,2,1,0:T(8,128)} %get-tuple-element.39) | data formatting | bytes 294912 | tf_op jit(solution)/shard_map/jit(kron)/mul | solution.py:114
  58.8 2.2 %collective-permute-done.4 = f32[5,8,14,1]{3,1,2,0:T(8,128)} collective-permute-done((f32[5,8,14,1]{3,1,2,0:T(8,128)S(1)}, f32[5,8,14,1]{3,1,2,0:T(8,128)}, u32[]{:S(2)}, u32[]{:S(2)}) %collective-permute-start.4) | collective-permute-done | bytes 2272 | tf_op jit(solution)/shard_map/ppermute | solution.py:25
  61.0 2.7 %fusion.55 = f32[5,12,192,6]{2,3,1,0:T(8,128)S(1)} fusion(f32[5,6,12,192]{3,1,2,0:T(8,128)S(1)} %fusion.3, f32[5,8,14,1]{3,1,2,0:T(8,128)} %collective-permute-done.5, f32[5,8,1,192]{3,1,2,0:T(8,128)S(1)} %collective-permute-done.2, f32[5,8,1,192]{3,1,2,0:T(8,128)S(1)} %collective-permute-done.3, f32[5,1,12,192]{3,1,2,0:T(1,128)S(1)} %collective-permute-done, ...), kind=kOutput, calls=%fused_computation.96 | convolution fusion | flops 7119360 | bytes 1476992 | tf_op jit(solution)/shard_map/...p,qp->...q/dot_general | solution.py:35
  67.9 1.3 collective-permute-start.6
  69.2 4.5 %collective-permute-start.7 = (f32[5,1,12,192]{3,1,2,0:T(1,128)S(1)}, f32[5,1,12,192]{3,1,2,0:T(1,128)S(1)}, u32[]{:S(2)}, u32[]{:S(2)}) collective-permute-start(f32[5,1,12,192]{3,1,2,0:T(1,128)S(1)} %get-tuple-element.20), channel_id=1, source_target_pairs={{0,16},{1,17},{2,18},{3,19},{4,20},{5,21},{6,22},{7,23},{8,24},{9,... | collective-permute-start | bytes 138248 | tf_op jit(solution)/shard_map/ppermute | solution.py:24
  74.4 1.2 collective-permute-done.7
  75.6 1.3 collective-permute-start.8
  76.9 3.3 %collective-permute-start.9 = (f32[5,8,1,192]{3,1,2,0:T(8,128)S(1)}, f32[5,8,1,192]{3,1,2,0:T(8,128)S(1)}, u32[]{:S(2)}, u32[]{:S(2)}) collective-permute-start(f32[5,8,1,192]{3,1,2,0:T(8,128)S(1)} %get-tuple-element.12), channel_id=1, source_target_pairs={{0,4},{4,8},{8,12},{1,5},{5,9},{9,13},{2,6},{6,10},{10,14},{3,7},{... | collective-permute-start | bytes 92168 | tf_op jit(solution)/shard_map/ppermute | solution.py:24
  81.4 2.4 %collective-permute-start.11 = (f32[5,8,14,1]{3,1,2,0:T(8,128)S(1)}, f32[5,8,14,1]{3,1,2,0:T(8,128)S(1)}, u32[]{:S(2)}, u32[]{:S(2)}) collective-permute-start(f32[5,8,14,1]{3,1,2,0:T(8,128)S(1)} %get-tuple-element.17), channel_id=1, source_target_pairs={{0,1},{1,2},{2,3},{4,5},{5,6},{6,7},{8,9},{9,10},{10,11},{12,13},{... | collective-permute-start | bytes 6728 | tf_op jit(solution)/shard_map/ppermute | solution.py:24
  83.8 1.3 collective-permute-start.10
  85.9 2.9 %collective-permute-done.11 = f32[5,8,14,1]{3,1,2,0:T(8,128)S(1)} collective-permute-done((f32[5,8,14,1]{3,1,2,0:T(8,128)S(1)}, f32[5,8,14,1]{3,1,2,0:T(8,128)S(1)}, u32[]{:S(2)}, u32[]{:S(2)}) %collective-permute-start.11) | collective-permute-done | bytes 2272 | tf_op jit(solution)/shard_map/ppermute | solution.py:24
  88.8 4.7 %collective-permute-done.10 = f32[5,8,14,1]{3,1,2,0:T(8,128)S(1)} collective-permute-done((f32[5,8,14,1]{3,1,2,0:T(8,128)S(1)}, f32[5,8,14,1]{3,1,2,0:T(8,128)S(1)}, u32[]{:S(2)}, u32[]{:S(2)}) %collective-permute-start.10) | collective-permute-done | bytes 2272 | tf_op jit(solution)/shard_map/ppermute | solution.py:25
  93.5 1.7 %fusion.28 = f32[5,12,192,6]{2,3,1,0:T(8,128)S(1)} fusion(f32[5,6,12,192]{3,1,2,0:T(8,128)S(1)} %fusion.7, f32[5,8,14,1]{3,1,2,0:T(8,128)S(1)} %collective-permute-done.11, f32[5,8,1,192]{3,1,2,0:T(8,128)S(1)} %collective-permute-done.8, f32[5,8,1,192]{3,1,2,0:T(8,128)S(1)} %collective-permute-done.9, f32[5,1,12,192]{3,1,2,0:T(1,128)S(1)} %collective-permute-done.6, ...), kind=kOutput, calls=%fused_computation.57 | convolution fusion | flops 7119360 | bytes 2045952 | tf_op jit(solution)/shard_map/...p,qp->...q/dot_general | solution.py:35
  99.0 0.9 copy.174
  100.2 14.4 %all_gather.7 = f32[4,16,128]{1,0,2:T(4,128)S(1)} all-gather(f32[4,16,32]{1,0,2:T(4,128)S(1)} %pad_maximum_fusion.62), channel_id=1, replica_groups=mesh['flow'=2,'col'=4,'row'=4] {'row'}, dimensions={2}, use_global_device_ids=true | all-gather | bytes 40960 | tf_op jit(solution)/shard_map/all_gather | solution.py:159
  115.4 2.7 %fusion.17 = (f32[16,64]{1,0:T(8,128)S(1)}, f32[16,64]{1,0:T(8,128)S(1)}) fusion(f32[16,128]{1,0:T(8,128)S(1)} %get-tuple-element.36, f32[64,128]{1,0:T(8,128)S(1)} %copy-done.6, f32[64,128]{1,0:T(8,128)S(1)} %copy-done.7, f32[16,128]{1,0:T(8,128)S(1)} %get-tuple-element.37, f32[16,128]{1,0:T(8,128)S(1)} %get-tuple-element.38, ...), kind=kLoop, calls=%fused_computation.41 | loop fusion | flops 3799040 | bytes 303232 | tf_op jit(solution)/shard_map/reduce_sum | solution.py:76
  118.1 25.7 %psum.7 = f32[2,16,64]{2,1,0:T(8,128)} all-reduce(f32[2,16,64]{2,1,0:T(8,128)S(1)} %pad_maximum_fusion.69), channel_id=1, replica_groups=mesh['flow'=2,'col'=4,'row'=4] {'flow','col'}, use_global_device_ids=true, to_apply=%region_3.4 | all-reduce | flops 2048 | bytes 16384 | tf_op jit(solution)/shard_map/psum | solution.py:164
  (102 shorter events, 18.2 us)
Async XLA Ops:
  0.6 35.6 %copy-start = (f32[3,256]{1,0:T(4,128)S(1)}, f32[3,256]{1,0:T(4,128)}, u32[]{:S(2)}) copy-start(f32[3,256]{1,0:T(4,128)} %param.13) | copy-start | bytes 9220
  1.7 38.0 %collective-permute-start = (f32[5,1,12,192]{3,1,2,0:T(1,128)S(1)}, f32[5,1,12,192]{3,1,2,0:T(1,128)S(1)}, u32[]{:S(2)}, u32[]{:S(2)}) collective-permute-start(f32[5,1,12,192]{3,1,2,0:T(1,128)S(1)} %copy.137), channel_id=1, source_target_pairs={{16,0},{17,1},{18,2},{19,3},{20,4},{21,5},{22,6},{23,7},{24,8},{25... | collective-permute-start | bytes 138248 | tf_op jit(solution)/shard_map/ppermute | solution.py:25
  3.0 36.6 %collective-permute-start.1 = (f32[5,1,12,192]{3,1,2,0:T(1,128)S(1)}, f32[5,1,12,192]{3,1,2,0:T(1,128)S(1)}, u32[]{:S(2)}, u32[]{:S(2)}) collective-permute-start(f32[5,1,12,192]{3,1,2,0:T(1,128)S(1)} %copy.139), channel_id=1, source_target_pairs={{0,16},{1,17},{2,18},{3,19},{4,20},{5,21},{6,22},{7,23},{8,24},{9,... | collective-permute-start | bytes 138248 | tf_op jit(solution)/shard_map/ppermute | solution.py:24
  16.6 4.0 %copy-start.1 = (f32[5,6,12,192]{3,2,1,0:T(8,128)S(1)}, f32[5,6,12,192]{3,2,1,0:T(8,128)}, u32[]{:S(2)}) copy-start(f32[5,6,12,192]{3,2,1,0:T(8,128)} %param.9) | copy-start | bytes 829444
  16.6 4.7 %copy-start.3 = (f32[3,6,6]{2,1,0:T(8,128)S(1)}, f32[3,6,6]{2,1,0:T(8,128)}, u32[]{:S(2)}) copy-start(f32[3,6,6]{2,1,0:T(8,128)} %param.11) | copy-start | bytes 1300
  16.6 5.8 %copy-start.13 = (f32[1,2,32]{2,1,0:T(2,128)S(1)}, f32[1,2,32]{2,1,0:T(2,128)}, u32[]{:S(2)}) copy-start(f32[1,2,32]{2,1,0:T(2,128)} %param.10) | copy-start | bytes 772
  16.6 6.3 %copy-start.12 = (f32[3,32]{1,0:T(4,128)S(1)}, f32[3,32]{1,0:T(4,128)}, u32[]{:S(2)}) copy-start(f32[3,32]{1,0:T(4,128)} %param.14) | copy-start | bytes 1156
  16.6 21.9 %copy-start.2 = (f32[5,6,12,192]{3,2,1,0:T(8,128)S(1)}, f32[5,6,12,192]{3,2,1,0:T(8,128)}, u32[]{:S(2)}) copy-start(f32[5,6,12,192]{3,2,1,0:T(8,128)} %param.8) | copy-start | bytes 829444
  39.7 4.4 %collective-permute-start.2 = (f32[5,8,1,192]{3,1,2,0:T(8,128)S(1)}, f32[5,8,1,192]{3,1,2,0:T(8,128)S(1)}, u32[]{:S(2)}, u32[]{:S(2)}) collective-permute-start(f32[5,8,1,192]{3,1,2,0:T(8,128)S(1)} %get-tuple-element.15), channel_id=1, source_target_pairs={{4,0},{8,4},{12,8},{5,1},{9,5},{13,9},{6,2},{10,6},{14,10},{7,3},{... | collective-permute-start | bytes 92168 | tf_op jit(solution)/shard_map/ppermute | solution.py:25
  41.0 3.9 %collective-permute-start.3 = (f32[5,8,1,192]{3,1,2,0:T(8,128)S(1)}, f32[5,8,1,192]{3,1,2,0:T(8,128)S(1)}, u32[]{:S(2)}, u32[]{:S(2)}) collective-permute-start(f32[5,8,1,192]{3,1,2,0:T(8,128)S(1)} %get-tuple-element.14), channel_id=1, source_target_pairs={{0,4},{4,8},{8,12},{1,5},{5,9},{9,13},{2,6},{6,10},{10,14},{3,7},{... | collective-permute-start | bytes 92168 | tf_op jit(solution)/shard_map/ppermute | solution.py:24
  45.3 13.6 %collective-permute-start.5 = (f32[5,8,14,1]{3,1,2,0:T(8,128)S(1)}, f32[5,8,14,1]{3,1,2,0:T(8,128)}, u32[]{:S(2)}, u32[]{:S(2)}) collective-permute-start(f32[5,8,14,1]{3,1,2,0:T(8,128)S(1)} %get-tuple-element.19), channel_id=1, source_target_pairs={{0,1},{1,2},{2,3},{4,5},{5,6},{6,7},{8,9},{9,10},{10,11},{12,13},{... | collective-permute-start | bytes 6728 | tf_op jit(solution)/shard_map/ppermute | solution.py:24
  49.5 11.6 %collective-permute-start.4 = (f32[5,8,14,1]{3,1,2,0:T(8,128)S(1)}, f32[5,8,14,1]{3,1,2,0:T(8,128)}, u32[]{:S(2)}, u32[]{:S(2)}) collective-permute-start(f32[5,8,14,1]{3,1,2,0:T(8,128)S(1)} %get-tuple-element.18), channel_id=1, source_target_pairs={{1,0},{2,1},{3,2},{5,4},{6,5},{7,6},{9,8},{10,9},{11,10},{13,12},{... | collective-permute-start | bytes 6728 | tf_op jit(solution)/shard_map/ppermute | solution.py:25
  51.0 7.7 %copy-start.11 = (f32[4,15,32]{2,0,1:T(4,128)S(1)}, f32[4,15,32]{2,0,1:T(4,128)}, u32[]{:S(2)}) copy-start(f32[4,15,32]{2,0,1:T(4,128)} %param.15) | copy-start | bytes 23044
  61.0 3.6 %copy-start.4 = (f32[6,12,192]{2,1,0:T(8,128)S(1)}, f32[6,12,192]{2,1,0:T(8,128)}, u32[]{:S(2)}) copy-start(f32[6,12,192]{2,1,0:T(8,128)} %add_add_fusion) | copy-start | bytes 165892
  67.9 6.5 %collective-permute-start.6 = (f32[5,1,12,192]{3,1,2,0:T(1,128)S(1)}, f32[5,1,12,192]{3,1,2,0:T(1,128)S(1)}, u32[]{:S(2)}, u32[]{:S(2)}) collective-permute-start(f32[5,1,12,192]{3,1,2,0:T(1,128)S(1)} %get-tuple-element.21), channel_id=1, source_target_pairs={{16,0},{17,1},{18,2},{19,3},{20,4},{21,5},{22,6},{23,7},{24,8},{25... | collective-permute-start | bytes 138248 | tf_op jit(solution)/shard_map/ppermute | solution.py:25
  69.2 6.4 %collective-permute-start.7 = (f32[5,1,12,192]{3,1,2,0:T(1,128)S(1)}, f32[5,1,12,192]{3,1,2,0:T(1,128)S(1)}, u32[]{:S(2)}, u32[]{:S(2)}) collective-permute-start(f32[5,1,12,192]{3,1,2,0:T(1,128)S(1)} %get-tuple-element.20), channel_id=1, source_target_pairs={{0,16},{1,17},{2,18},{3,19},{4,20},{5,21},{6,22},{7,23},{8,24},{9,... | collective-permute-start | bytes 138248 | tf_op jit(solution)/shard_map/ppermute | solution.py:24
  75.6 5.4 %collective-permute-start.8 = (f32[5,8,1,192]{3,1,2,0:T(8,128)S(1)}, f32[5,8,1,192]{3,1,2,0:T(8,128)S(1)}, u32[]{:S(2)}, u32[]{:S(2)}) collective-permute-start(f32[5,8,1,192]{3,1,2,0:T(8,128)S(1)} %get-tuple-element.13), channel_id=1, source_target_pairs={{4,0},{8,4},{12,8},{5,1},{9,5},{13,9},{6,2},{10,6},{14,10},{7,3},{... | collective-permute-start | bytes 92168 | tf_op jit(solution)/shard_map/ppermute | solution.py:25
  76.9 4.1 %collective-permute-start.9 = (f32[5,8,1,192]{3,1,2,0:T(8,128)S(1)}, f32[5,8,1,192]{3,1,2,0:T(8,128)S(1)}, u32[]{:S(2)}, u32[]{:S(2)}) collective-permute-start(f32[5,8,1,192]{3,1,2,0:T(8,128)S(1)} %get-tuple-element.12), channel_id=1, source_target_pairs={{0,4},{4,8},{8,12},{1,5},{5,9},{9,13},{2,6},{6,10},{10,14},{3,7},{... | collective-permute-start | bytes 92168 | tf_op jit(solution)/shard_map/ppermute | solution.py:24
  81.4 7.4 %collective-permute-start.11 = (f32[5,8,14,1]{3,1,2,0:T(8,128)S(1)}, f32[5,8,14,1]{3,1,2,0:T(8,128)S(1)}, u32[]{:S(2)}, u32[]{:S(2)}) collective-permute-start(f32[5,8,14,1]{3,1,2,0:T(8,128)S(1)} %get-tuple-element.17), channel_id=1, source_target_pairs={{0,1},{1,2},{2,3},{4,5},{5,6},{6,7},{8,9},{9,10},{10,11},{12,13},{... | collective-permute-start | bytes 6728 | tf_op jit(solution)/shard_map/ppermute | solution.py:24
  83.8 9.7 %collective-permute-start.10 = (f32[5,8,14,1]{3,1,2,0:T(8,128)S(1)}, f32[5,8,14,1]{3,1,2,0:T(8,128)S(1)}, u32[]{:S(2)}, u32[]{:S(2)}) collective-permute-start(f32[5,8,14,1]{3,1,2,0:T(8,128)S(1)} %get-tuple-element.16), channel_id=1, source_target_pairs={{1,0},{2,1},{3,2},{5,4},{6,5},{7,6},{9,8},{10,9},{11,10},{13,12},{... | collective-permute-start | bytes 6728 | tf_op jit(solution)/shard_map/ppermute | solution.py:25
  97.4 17.9 %copy-start.5 = (f32[64,128]{1,0:T(8,128)S(1)}, f32[64,128]{1,0:T(8,128)}, u32[]{:S(2)}) copy-start(f32[64,128]{1,0:T(8,128)} %get-tuple-element.27) | copy-start | bytes 98308
  97.4 17.9 %copy-start.6 = (f32[64,128]{1,0:T(8,128)S(1)}, f32[64,128]{1,0:T(8,128)}, u32[]{:S(2)}) copy-start(f32[64,128]{1,0:T(8,128)} %get-tuple-element.28) | copy-start | bytes 98308
  97.4 17.9 %copy-start.7 = (f32[64,128]{1,0:T(8,128)S(1)}, f32[64,128]{1,0:T(8,128)}, u32[]{:S(2)}) copy-start(f32[64,128]{1,0:T(8,128)} %get-tuple-element.30) | copy-start | bytes 98308
  97.4 17.9 %copy-start.8 = (f32[64,128]{1,0:T(8,128)S(1)}, f32[64,128]{1,0:T(8,128)}, u32[]{:S(2)}) copy-start(f32[64,128]{1,0:T(8,128)} %get-tuple-element.24) | copy-start | bytes 98308
  97.5 17.9 %copy-start.9 = (f32[64,128]{1,0:T(8,128)S(1)}, f32[64,128]{1,0:T(8,128)}, u32[]{:S(2)}) copy-start(f32[64,128]{1,0:T(8,128)} %get-tuple-element.25) | copy-start | bytes 98308
  97.5 17.9 %copy-start.10 = (f32[64,128]{1,0:T(8,128)S(1)}, f32[64,128]{1,0:T(8,128)}, u32[]{:S(2)}) copy-start(f32[64,128]{1,0:T(8,128)} %get-tuple-element.26) | copy-start | bytes 98308
where the time goes:
time: 144 us
  blocking collectives  53.4 us (37%)
  starting transfers between devices  30.3 us (21%)
  local copies, waits for them, and re-layouts  19.8 us (14%)
  matrix products  17.4 us (12%)
  waiting for transfers between devices  11.9 us (8%)
  other arithmetic  9.8 us (7%)
    psum x1, blocking collectives, on_device(): spectra = lax.psum(partial_sums, ('flow', 'col'))  25.7 us
    ppermute x6, starting transfers between devices, with_halo(): before = lax.ppermute(last, axis, up)  22.3 us
    all_gather x1, blocking collectives, on_device(): lax.all_gather(surface_samples, 'row', axis=2, tiled=True)  14.4 us
    all_gather x1, blocking collectives, on_device(): lax.all_gather(panel_points, 'row', axis=1, tiled=True)  13.2 us
    dot_general x12, matrix products, contract_small(): result = jnp.einsum('...p,qp->...q', blocked, matrix, precision=HIGH)  11.6 us
    ppermute x6, starting transfers between devices, with_halo(): after = lax.ppermute(first, axis, down)  7.92 us
    ppermute x6, waiting for transfers between devices, with_halo(): after = lax.ppermute(first, axis, down)  6.94 us
    mul x1, other arithmetic, on_device(): wide_back = jnp.kron(identity, eigen_bases[2])  4.95 us
  transfers between devices with their start and end apart: 12, of which 5 were waited for; matrix products, arithmetic and copies ran while one was open for 20% of the time, Pallas kernels for 0%

commit v1 on v0

--- a/solution.py
+++ b/solution.py
@@ -161,7 +161,7 @@
     source_re, source_im = transform(samples)
     own_obs = lax.dynamic_slice_in_dim(observers, lax.axis_index("row") * count, count, 1)
     partial_sums = far_terms(own_obs, points, source_re, source_im)
-    spectra = lax.psum(partial_sums, ("flow", "col"))
+    spectra = jnp.sum(lax.all_gather(partial_sums, ("flow", "col")), axis=0)
     return (state, spectra)
 
 

time: 144 us -> 131 us (0.910)
  blocking collectives: 53.4 us -> 39.4 us
    psum x1 -> x0, blocking collectives: 25.7 us -> none  [on_device(): spectra = lax.psum(partial_sums, ('flow', 'col'))]
    all_gather x0 -> x1, blocking collectives: none -> 11.7 us  [on_device(): spectra = jnp.sum(lax.all_gather(partial_sums, ('flow', 'col')), axis=0)]
  transfers between devices with their start and end apart: 12 -> 12, of which waited for: 5 -> 5; matrix products, arithmetic and copies ran while one was open for 20% -> 22% of each run, Pallas kernels for 0% -> 0%
where the time goes in v1:
time: 131 us; the launch traced here: 130 us
  blocking collectives  39.4 us (30%)
  starting transfers between devices  30.3 us (23%)
  local copies, waits for them, and re-layouts  19.8 us (15%)
  matrix products  17.4 us (13%)
  waiting for transfers between devices  11.9 us (9%)
  other arithmetic  10.4 us (8%)
  between operations  1.33 us (1%)
    ppermute x6, starting transfers between devices, with_halo(): before = lax.ppermute(last, axis, up)  22.3 us
    all_gather x1, blocking collectives, on_device(): lax.all_gather(surface_samples, 'row', axis=2, tiled=True)  14.4 us
    all_gather x1, blocking collectives, on_device(): lax.all_gather(panel_points, 'row', axis=1, tiled=True)  13.2 us
    all_gather x1, blocking collectives, on_device(): spectra = jnp.sum(lax.all_gather(partial_sums, ('flow', 'col')), axis=0)  11.7 us
    dot_general x12, matrix products, contract_small(): result = jnp.einsum('...p,qp->...q', blocked, matrix, precision=HIGH)  11.6 us
    ppermute x6, starting transfers between devices, with_halo(): after = lax.ppermute(first, axis, down)  7.92 us
    ppermute x6, waiting for transfers between devices, with_halo(): after = lax.ppermute(first, axis, down)  6.94 us
    mul x1, other arithmetic, on_device(): wide_back = jnp.kron(identity, eigen_bases[2])  4.95 us
  transfers between devices with their start and end apart: 12, of which 5 were waited for; matrix products, arithmetic and copies ran while one was open for 22% of the time, Pallas kernels for 0%

profile of v1, /device:TPU:0, one launch (start us, length us, event | category | flops | bytes accessed | tf_op | source)
XLA Modules:
  0.0 130.4 jit_solution(9131583842818226557)
XLA Ops:
  0.6 0.9 fusion.168
  1.7 1.3 collective-permute-start
  3.0 4.8 %collective-permute-start.1 = (f32[5,1,12,192]{3,1,2,0:T(1,128)S(1)}, f32[5,1,12,192]{3,1,2,0:T(1,128)S(1)}, u32[]{:S(2)}, u32[]{:S(2)}) collective-permute-start(f32[5,1,12,192]{3,1,2,0:T(1,128)S(1)} %copy.139), channel_id=1, source_target_pairs={{0,16},{1,17},{2,18},{3,19},{4,20},{5,21},{6,22},{7,23},{8,24},{9,... | collective-permute-start | bytes 138248 | tf_op jit(solution)/shard_map/ppermute | solution.py:24
  7.9 1.3 copy.153
  10.8 0.9 fusion.131
  11.7 4.9 %broadcast_multiply_fusion = (f32[32,6,32,6]{3,2,1,0:T(8,128)}, f32[32,6,32,6]{3,2,1,0:T(8,128)}, f32[32,6,32,6]{3,2,1,0:T(8,128)}) fusion(f32[6,6]{1,0:T(8,128)S(1)} %get-tuple-element.42, f32[32,32]{1,0:T(8,128)S(1)} %fusion.118, f32[6,6]{1,0:T(8,128)S(1)} %copy.146, f32[6,6]{1,0:T(8,128)S(1)} %fusion.131), kind=kLoop, calls=%fused_computation | loop fusion | flops 110592 | bytes 446896 | tf_op jit(solution)/shard_map/jit(kron)/mul | solution.py:114
  16.6 3.9 %reshape.302 = f32[192,192,1,1]{1,0,2,3:T(8,128)S(1)} reshape(f32[32,6,32,6]{3,2,1,0:T(8,128)} %get-tuple-element.41) | data formatting | bytes 294912 | tf_op jit(solution)/shard_map/jit(kron)/mul | solution.py:112
  22.9 13.2 %all-gather.1 = f32[4,32,3]{1,2,0:T(4,128)S(1)} all-gather(f32[1,32,3]{1,2,0:T(4,128)S(1)} %bitcast.284), channel_id=1, replica_groups=mesh['flow'=2,'col'=4,'row'=4] {'row'}, dimensions={0}, use_global_device_ids=true | all-gather | bytes 1920 | tf_op jit(solution)/shard_map/all_gather | solution.py:158
  38.5 1.1 fusion.3
  39.7 1.3 collective-permute-start.2
  41.0 3.0 %collective-permute-start.3 = (f32[5,8,1,192]{3,1,2,0:T(8,128)S(1)}, f32[5,8,1,192]{3,1,2,0:T(8,128)S(1)}, u32[]{:S(2)}, u32[]{:S(2)}) collective-permute-start(f32[5,8,1,192]{3,1,2,0:T(8,128)S(1)} %get-tuple-element.14), channel_id=1, source_target_pairs={{0,4},{4,8},{8,12},{1,5},{5,9},{9,13},{2,6},{6,10},{10,14},{3,7},{... | collective-permute-start | bytes 92168 | tf_op jit(solution)/shard_map/ppermute | solution.py:24
  44.1 0.8 collective-permute-done.3
  45.3 4.2 %collective-permute-start.5 = (f32[5,8,14,1]{3,1,2,0:T(8,128)S(1)}, f32[5,8,14,1]{3,1,2,0:T(8,128)}, u32[]{:S(2)}, u32[]{:S(2)}) collective-permute-start(f32[5,8,14,1]{3,1,2,0:T(8,128)S(1)} %get-tuple-element.19), channel_id=1, source_target_pairs={{0,1},{1,2},{2,3},{4,5},{5,6},{6,7},{8,9},{9,10},{10,11},{12,13},{... | collective-permute-start | bytes 6728 | tf_op jit(solution)/shard_map/ppermute | solution.py:24
  49.5 1.5 %collective-permute-start.4 = (f32[5,8,14,1]{3,1,2,0:T(8,128)S(1)}, f32[5,8,14,1]{3,1,2,0:T(8,128)}, u32[]{:S(2)}, u32[]{:S(2)}) collective-permute-start(f32[5,8,14,1]{3,1,2,0:T(8,128)S(1)} %get-tuple-element.18), channel_id=1, source_target_pairs={{1,0},{2,1},{3,2},{5,4},{6,5},{7,6},{9,8},{10,9},{11,10},{13,12},{... | collective-permute-start | bytes 6728 | tf_op jit(solution)/shard_map/ppermute | solution.py:25
  51.0 3.9 %reshape.305 = f32[192,192,1,1]{1,0,2,3:T(8,128)S(1)} reshape(f32[32,6,32,6]{3,2,1,0:T(8,128)} %get-tuple-element.40) | data formatting | bytes 294912 | tf_op jit(solution)/shard_map/jit(kron)/mul | solution.py:113
  54.8 3.9 %reshape.308 = f32[192,192,1,1]{1,0,2,3:T(8,128)S(1)} reshape(f32[32,6,32,6]{3,2,1,0:T(8,128)} %get-tuple-element.39) | data formatting | bytes 294912 | tf_op jit(solution)/shard_map/jit(kron)/mul | solution.py:114
  58.8 2.2 %collective-permute-done.4 = f32[5,8,14,1]{3,1,2,0:T(8,128)} collective-permute-done((f32[5,8,14,1]{3,1,2,0:T(8,128)S(1)}, f32[5,8,14,1]{3,1,2,0:T(8,128)}, u32[]{:S(2)}, u32[]{:S(2)}) %collective-permute-start.4) | collective-permute-done | bytes 2272 | tf_op jit(solution)/shard_map/ppermute | solution.py:25
  61.0 2.7 %fusion.55 = f32[5,12,192,6]{2,3,1,0:T(8,128)S(1)} fusion(f32[5,6,12,192]{3,1,2,0:T(8,128)S(1)} %fusion.3, f32[5,8,14,1]{3,1,2,0:T(8,128)} %collective-permute-done.5, f32[5,8,1,192]{3,1,2,0:T(8,128)S(1)} %collective-permute-done.2, f32[5,8,1,192]{3,1,2,0:T(8,128)S(1)} %collective-permute-done.3, f32[5,1,12,192]{3,1,2,0:T(1,128)S(1)} %collective-permute-done, ...), kind=kOutput, calls=%fused_computation.96 | convolution fusion | flops 7119360 | bytes 1476992 | tf_op jit(solution)/shard_map/...p,qp->...q/dot_general | solution.py:35
  67.9 1.3 collective-permute-start.6
  69.2 4.5 %collective-permute-start.7 = (f32[5,1,12,192]{3,1,2,0:T(1,128)S(1)}, f32[5,1,12,192]{3,1,2,0:T(1,128)S(1)}, u32[]{:S(2)}, u32[]{:S(2)}) collective-permute-start(f32[5,1,12,192]{3,1,2,0:T(1,128)S(1)} %get-tuple-element.20), channel_id=1, source_target_pairs={{0,16},{1,17},{2,18},{3,19},{4,20},{5,21},{6,22},{7,23},{8,24},{9,... | collective-permute-start | bytes 138248 | tf_op jit(solution)/shard_map/ppermute | solution.py:24
  74.4 1.2 collective-permute-done.7
  75.6 1.3 collective-permute-start.8
  76.9 3.3 %collective-permute-start.9 = (f32[5,8,1,192]{3,1,2,0:T(8,128)S(1)}, f32[5,8,1,192]{3,1,2,0:T(8,128)S(1)}, u32[]{:S(2)}, u32[]{:S(2)}) collective-permute-start(f32[5,8,1,192]{3,1,2,0:T(8,128)S(1)} %get-tuple-element.12), channel_id=1, source_target_pairs={{0,4},{4,8},{8,12},{1,5},{5,9},{9,13},{2,6},{6,10},{10,14},{3,7},{... | collective-permute-start | bytes 92168 | tf_op jit(solution)/shard_map/ppermute | solution.py:24
  81.4 2.4 %collective-permute-start.11 = (f32[5,8,14,1]{3,1,2,0:T(8,128)S(1)}, f32[5,8,14,1]{3,1,2,0:T(8,128)S(1)}, u32[]{:S(2)}, u32[]{:S(2)}) collective-permute-start(f32[5,8,14,1]{3,1,2,0:T(8,128)S(1)} %get-tuple-element.17), channel_id=1, source_target_pairs={{0,1},{1,2},{2,3},{4,5},{5,6},{6,7},{8,9},{9,10},{10,11},{12,13},{... | collective-permute-start | bytes 6728 | tf_op jit(solution)/shard_map/ppermute | solution.py:24
  83.8 1.3 collective-permute-start.10
  85.9 2.9 %collective-permute-done.11 = f32[5,8,14,1]{3,1,2,0:T(8,128)S(1)} collective-permute-done((f32[5,8,14,1]{3,1,2,0:T(8,128)S(1)}, f32[5,8,14,1]{3,1,2,0:T(8,128)S(1)}, u32[]{:S(2)}, u32[]{:S(2)}) %collective-permute-start.11) | collective-permute-done | bytes 2272 | tf_op jit(solution)/shard_map/ppermute | solution.py:24
  88.8 4.7 %collective-permute-done.10 = f32[5,8,14,1]{3,1,2,0:T(8,128)S(1)} collective-permute-done((f32[5,8,14,1]{3,1,2,0:T(8,128)S(1)}, f32[5,8,14,1]{3,1,2,0:T(8,128)S(1)}, u32[]{:S(2)}, u32[]{:S(2)}) %collective-permute-start.10) | collective-permute-done | bytes 2272 | tf_op jit(solution)/shard_map/ppermute | solution.py:25
  93.5 1.7 %fusion.28 = f32[5,12,192,6]{2,3,1,0:T(8,128)S(1)} fusion(f32[5,6,12,192]{3,1,2,0:T(8,128)S(1)} %fusion.7, f32[5,8,14,1]{3,1,2,0:T(8,128)S(1)} %collective-permute-done.11, f32[5,8,1,192]{3,1,2,0:T(8,128)S(1)} %collective-permute-done.8, f32[5,8,1,192]{3,1,2,0:T(8,128)S(1)} %collective-permute-done.9, f32[5,1,12,192]{3,1,2,0:T(1,128)S(1)} %collective-permute-done.6, ...), kind=kOutput, calls=%fused_computation.57 | convolution fusion | flops 7119360 | bytes 2045952 | tf_op jit(solution)/shard_map/...p,qp->...q/dot_general | solution.py:35
  99.0 0.9 copy.174
  100.2 14.4 %all_gather.13 = f32[4,16,128]{1,0,2:T(4,128)S(1)} all-gather(f32[4,16,32]{1,0,2:T(4,128)S(1)} %pad_maximum_fusion.62), channel_id=1, replica_groups=mesh['flow'=2,'col'=4,'row'=4] {'row'}, dimensions={2}, use_global_device_ids=true | all-gather | bytes 40960 | tf_op jit(solution)/shard_map/all_gather | solution.py:159
  115.4 2.7 %fusion.17 = (f32[16,64]{1,0:T(8,128)S(1)}, f32[16,64]{1,0:T(8,128)S(1)}) fusion(f32[16,128]{1,0:T(8,128)S(1)} %get-tuple-element.36, f32[64,128]{1,0:T(8,128)S(1)} %copy-done.6, f32[64,128]{1,0:T(8,128)S(1)} %copy-done.7, f32[16,128]{1,0:T(8,128)S(1)} %get-tuple-element.37, f32[16,128]{1,0:T(8,128)S(1)} %get-tuple-element.38, ...), kind=kLoop, calls=%fused_computation.41 | loop fusion | flops 3799040 | bytes 303232 | tf_op jit(solution)/shard_map/reduce_sum | solution.py:76
  118.1 11.7 %all-gather = f32[16,16,64]{2,1,0:T(8,128)S(1)} all-gather(f32[2,16,64]{2,1,0:T(8,128)S(1)} %pad_maximum_fusion.69), channel_id=2, replica_groups=mesh['flow'=2,'col'=4,'row'=4] {'flow','col'}, dimensions={0}, use_global_device_ids=true | all-gather | bytes 73728 | tf_op jit(solution)/shard_map/all_gather | solution.py:164
  (103 shorter events, 18.8 us)
Async XLA Ops:
  0.6 35.6 %copy-start = (f32[3,256]{1,0:T(4,128)S(1)}, f32[3,256]{1,0:T(4,128)}, u32[]{:S(2)}) copy-start(f32[3,256]{1,0:T(4,128)} %param.13) | copy-start | bytes 9220
  1.7 38.0 %collective-permute-start = (f32[5,1,12,192]{3,1,2,0:T(1,128)S(1)}, f32[5,1,12,192]{3,1,2,0:T(1,128)S(1)}, u32[]{:S(2)}, u32[]{:S(2)}) collective-permute-start(f32[5,1,12,192]{3,1,2,0:T(1,128)S(1)} %copy.137), channel_id=1, source_target_pairs={{16,0},{17,1},{18,2},{19,3},{20,4},{21,5},{22,6},{23,7},{24,8},{25... | collective-permute-start | bytes 138248 | tf_op jit(solution)/shard_map/ppermute | solution.py:25
  3.0 36.6 %collective-permute-start.1 = (f32[5,1,12,192]{3,1,2,0:T(1,128)S(1)}, f32[5,1,12,192]{3,1,2,0:T(1,128)S(1)}, u32[]{:S(2)}, u32[]{:S(2)}) collective-permute-start(f32[5,1,12,192]{3,1,2,0:T(1,128)S(1)} %copy.139), channel_id=1, source_target_pairs={{0,16},{1,17},{2,18},{3,19},{4,20},{5,21},{6,22},{7,23},{8,24},{9,... | collective-permute-start | bytes 138248 | tf_op jit(solution)/shard_map/ppermute | solution.py:24
  16.6 4.0 %copy-start.1 = (f32[5,6,12,192]{3,2,1,0:T(8,128)S(1)}, f32[5,6,12,192]{3,2,1,0:T(8,128)}, u32[]{:S(2)}) copy-start(f32[5,6,12,192]{3,2,1,0:T(8,128)} %param.9) | copy-start | bytes 829444
  16.6 4.7 %copy-start.3 = (f32[3,6,6]{2,1,0:T(8,128)S(1)}, f32[3,6,6]{2,1,0:T(8,128)}, u32[]{:S(2)}) copy-start(f32[3,6,6]{2,1,0:T(8,128)} %param.11) | copy-start | bytes 1300
  16.6 5.8 %copy-start.13 = (f32[1,2,32]{2,1,0:T(2,128)S(1)}, f32[1,2,32]{2,1,0:T(2,128)}, u32[]{:S(2)}) copy-start(f32[1,2,32]{2,1,0:T(2,128)} %param.10) | copy-start | bytes 772
  16.6 6.3 %copy-start.12 = (f32[3,32]{1,0:T(4,128)S(1)}, f32[3,32]{1,0:T(4,128)}, u32[]{:S(2)}) copy-start(f32[3,32]{1,0:T(4,128)} %param.14) | copy-start | bytes 1156
  16.6 21.9 %copy-start.2 = (f32[5,6,12,192]{3,2,1,0:T(8,128)S(1)}, f32[5,6,12,192]{3,2,1,0:T(8,128)}, u32[]{:S(2)}) copy-start(f32[5,6,12,192]{3,2,1,0:T(8,128)} %param.8) | copy-start | bytes 829444
  39.7 4.4 %collective-permute-start.2 = (f32[5,8,1,192]{3,1,2,0:T(8,128)S(1)}, f32[5,8,1,192]{3,1,2,0:T(8,128)S(1)}, u32[]{:S(2)}, u32[]{:S(2)}) collective-permute-start(f32[5,8,1,192]{3,1,2,0:T(8,128)S(1)} %get-tuple-element.15), channel_id=1, source_target_pairs={{4,0},{8,4},{12,8},{5,1},{9,5},{13,9},{6,2},{10,6},{14,10},{7,3},{... | collective-permute-start | bytes 92168 | tf_op jit(solution)/shard_map/ppermute | solution.py:25
  41.0 3.9 %collective-permute-start.3 = (f32[5,8,1,192]{3,1,2,0:T(8,128)S(1)}, f32[5,8,1,192]{3,1,2,0:T(8,128)S(1)}, u32[]{:S(2)}, u32[]{:S(2)}) collective-permute-start(f32[5,8,1,192]{3,1,2,0:T(8,128)S(1)} %get-tuple-element.14), channel_id=1, source_target_pairs={{0,4},{4,8},{8,12},{1,5},{5,9},{9,13},{2,6},{6,10},{10,14},{3,7},{... | collective-permute-start | bytes 92168 | tf_op jit(solution)/shard_map/ppermute | solution.py:24
  45.3 13.6 %collective-permute-start.5 = (f32[5,8,14,1]{3,1,2,0:T(8,128)S(1)}, f32[5,8,14,1]{3,1,2,0:T(8,128)}, u32[]{:S(2)}, u32[]{:S(2)}) collective-permute-start(f32[5,8,14,1]{3,1,2,0:T(8,128)S(1)} %get-tuple-element.19), channel_id=1, source_target_pairs={{0,1},{1,2},{2,3},{4,5},{5,6},{6,7},{8,9},{9,10},{10,11},{12,13},{... | collective-permute-start | bytes 6728 | tf_op jit(solution)/shard_map/ppermute | solution.py:24
  49.5 11.6 %collective-permute-start.4 = (f32[5,8,14,1]{3,1,2,0:T(8,128)S(1)}, f32[5,8,14,1]{3,1,2,0:T(8,128)}, u32[]{:S(2)}, u32[]{:S(2)}) collective-permute-start(f32[5,8,14,1]{3,1,2,0:T(8,128)S(1)} %get-tuple-element.18), channel_id=1, source_target_pairs={{1,0},{2,1},{3,2},{5,4},{6,5},{7,6},{9,8},{10,9},{11,10},{13,12},{... | collective-permute-start | bytes 6728 | tf_op jit(solution)/shard_map/ppermute | solution.py:25
  51.0 7.7 %copy-start.11 = (f32[4,15,32]{2,0,1:T(4,128)S(1)}, f32[4,15,32]{2,0,1:T(4,128)}, u32[]{:S(2)}) copy-start(f32[4,15,32]{2,0,1:T(4,128)} %param.15) | copy-start | bytes 23044
  61.0 3.6 %copy-start.4 = (f32[6,12,192]{2,1,0:T(8,128)S(1)}, f32[6,12,192]{2,1,0:T(8,128)}, u32[]{:S(2)}) copy-start(f32[6,12,192]{2,1,0:T(8,128)} %add_add_fusion) | copy-start | bytes 165892
  67.9 6.5 %collective-permute-start.6 = (f32[5,1,12,192]{3,1,2,0:T(1,128)S(1)}, f32[5,1,12,192]{3,1,2,0:T(1,128)S(1)}, u32[]{:S(2)}, u32[]{:S(2)}) collective-permute-start(f32[5,1,12,192]{3,1,2,0:T(1,128)S(1)} %get-tuple-element.21), channel_id=1, source_target_pairs={{16,0},{17,1},{18,2},{19,3},{20,4},{21,5},{22,6},{23,7},{24,8},{25... | collective-permute-start | bytes 138248 | tf_op jit(solution)/shard_map/ppermute | solution.py:25
  69.2 6.4 %collective-permute-start.7 = (f32[5,1,12,192]{3,1,2,0:T(1,128)S(1)}, f32[5,1,12,192]{3,1,2,0:T(1,128)S(1)}, u32[]{:S(2)}, u32[]{:S(2)}) collective-permute-start(f32[5,1,12,192]{3,1,2,0:T(1,128)S(1)} %get-tuple-element.20), channel_id=1, source_target_pairs={{0,16},{1,17},{2,18},{3,19},{4,20},{5,21},{6,22},{7,23},{8,24},{9,... | collective-permute-start | bytes 138248 | tf_op jit(solution)/shard_map/ppermute | solution.py:24
  75.6 5.4 %collective-permute-start.8 = (f32[5,8,1,192]{3,1,2,0:T(8,128)S(1)}, f32[5,8,1,192]{3,1,2,0:T(8,128)S(1)}, u32[]{:S(2)}, u32[]{:S(2)}) collective-permute-start(f32[5,8,1,192]{3,1,2,0:T(8,128)S(1)} %get-tuple-element.13), channel_id=1, source_target_pairs={{4,0},{8,4},{12,8},{5,1},{9,5},{13,9},{6,2},{10,6},{14,10},{7,3},{... | collective-permute-start | bytes 92168 | tf_op jit(solution)/shard_map/ppermute | solution.py:25
  76.9 4.1 %collective-permute-start.9 = (f32[5,8,1,192]{3,1,2,0:T(8,128)S(1)}, f32[5,8,1,192]{3,1,2,0:T(8,128)S(1)}, u32[]{:S(2)}, u32[]{:S(2)}) collective-permute-start(f32[5,8,1,192]{3,1,2,0:T(8,128)S(1)} %get-tuple-element.12), channel_id=1, source_target_pairs={{0,4},{4,8},{8,12},{1,5},{5,9},{9,13},{2,6},{6,10},{10,14},{3,7},{... | collective-permute-start | bytes 92168 | tf_op jit(solution)/shard_map/ppermute | solution.py:24
  81.4 7.4 %collective-permute-start.11 = (f32[5,8,14,1]{3,1,2,0:T(8,128)S(1)}, f32[5,8,14,1]{3,1,2,0:T(8,128)S(1)}, u32[]{:S(2)}, u32[]{:S(2)}) collective-permute-start(f32[5,8,14,1]{3,1,2,0:T(8,128)S(1)} %get-tuple-element.17), channel_id=1, source_target_pairs={{0,1},{1,2},{2,3},{4,5},{5,6},{6,7},{8,9},{9,10},{10,11},{12,13},{... | collective-permute-start | bytes 6728 | tf_op jit(solution)/shard_map/ppermute | solution.py:24
  83.8 9.7 %collective-permute-start.10 = (f32[5,8,14,1]{3,1,2,0:T(8,128)S(1)}, f32[5,8,14,1]{3,1,2,0:T(8,128)S(1)}, u32[]{:S(2)}, u32[]{:S(2)}) collective-permute-start(f32[5,8,14,1]{3,1,2,0:T(8,128)S(1)} %get-tuple-element.16), channel_id=1, source_target_pairs={{1,0},{2,1},{3,2},{5,4},{6,5},{7,6},{9,8},{10,9},{11,10},{13,12},{... | collective-permute-start | bytes 6728 | tf_op jit(solution)/shard_map/ppermute | solution.py:25
  97.4 17.9 %copy-start.5 = (f32[64,128]{1,0:T(8,128)S(1)}, f32[64,128]{1,0:T(8,128)}, u32[]{:S(2)}) copy-start(f32[64,128]{1,0:T(8,128)} %get-tuple-element.27) | copy-start | bytes 98308
  97.4 17.9 %copy-start.6 = (f32[64,128]{1,0:T(8,128)S(1)}, f32[64,128]{1,0:T(8,128)}, u32[]{:S(2)}) copy-start(f32[64,128]{1,0:T(8,128)} %get-tuple-element.28) | copy-start | bytes 98308
  97.4 17.9 %copy-start.7 = (f32[64,128]{1,0:T(8,128)S(1)}, f32[64,128]{1,0:T(8,128)}, u32[]{:S(2)}) copy-start(f32[64,128]{1,0:T(8,128)} %get-tuple-element.30) | copy-start | bytes 98308
  97.4 17.9 %copy-start.8 = (f32[64,128]{1,0:T(8,128)S(1)}, f32[64,128]{1,0:T(8,128)}, u32[]{:S(2)}) copy-start(f32[64,128]{1,0:T(8,128)} %get-tuple-element.24) | copy-start | bytes 98308
  97.5 17.9 %copy-start.9 = (f32[64,128]{1,0:T(8,128)S(1)}, f32[64,128]{1,0:T(8,128)}, u32[]{:S(2)}) copy-start(f32[64,128]{1,0:T(8,128)} %get-tuple-element.25) | copy-start | bytes 98308
  97.5 17.9 %copy-start.10 = (f32[64,128]{1,0:T(8,128)S(1)}, f32[64,128]{1,0:T(8,128)}, u32[]{:S(2)}) copy-start(f32[64,128]{1,0:T(8,128)} %get-tuple-element.26) | copy-start | bytes 98308
